TPU v7x, 32 devices: a whole 2x2x4 slice. The times are simulated.
32 devices in a mesh: leaf: 8 (over z, x), sep: 4 (over y, core).
Axes of the slice: x: 2, y: 2, z: 4, core: 2. Of those that a mesh axis runs over, the one named last changes fastest.
Arguments:
- right_side: float32 [32768, 128], P(('leaf', 'sep')), may hold values from -6 to 6
- inverse_root: bfloat16 [8192, 8192], P(('leaf', 'sep')), may hold values from -1 to 3
- inverse_middle: bfloat16 [8192, 4096], P(('leaf', 'sep')), may hold values from -1 to 3
- inverse_lower: bfloat16 [16384, 4096], P(('leaf', 'sep')), may hold values from -1 to 3
- update_middle: bfloat16 [8192, 128], P(('leaf', 'sep')), may hold values from -0.09375 to 0.09375
- update_lower: bfloat16 [16384, 64], P(('leaf', 'sep')), may hold values from -0.09375 to 0.09375
- target_middle: int32 [32, 1], P(('leaf', 'sep')), may hold values from 0 to 31
- target_lower: int32 [32, 1], P(('leaf', 'sep')), may hold values from 0 to 63
Outputs:
- solution: float32 [32768, 128], P(('leaf', 'sep'))
All inputs are finite; a program needn't handle non-finite values.
Results may differ from a plain program's by a relative error of at most 0.0037.
Values may be sent and summed in bfloat16 or wider, within the bound.
A program may use at most 64 MiB of HBM per device.

v0:
```python
import jax
import jax.numpy as jnp
from jax import lax
from jax.sharding import PartitionSpec as P

BLOCK = 8


def from_partner(block, axis, distance):
    count = lax.axis_size(axis)
    route = []
    for low in range(count):
        high = low | 1 << distance
        if high != low and high < count:
            route += [(low, high), (high, low)]
    return lax.ppermute(block, axis, route)


def on_device(
    right_side,
    inverse_root,
    inverse_middle,
    inverse_lower,
    update_middle,
    update_lower,
    target_middle,
    target_lower,
):
    leaf_index = lax.axis_index("leaf")
    leaf_count = lax.axis_size("leaf")
    leaf_bits = leaf_count.bit_length() - 1
    dev_rows = inverse_root.shape[0]
    width = right_side.shape[1]
    root_side = right_side[:dev_rows]
    middle_side = right_side[dev_rows : 2 * dev_rows]
    lower_side = right_side[2 * dev_rows :]

    def collect(piece, depth_bits):
        panel = lax.all_gather(piece, "sep", axis=0, tiled=True)
        for bit_index in range(depth_bits):
            partner = from_partner(panel, "leaf", bit_index)
            upper = leaf_index >> bit_index & 1 == 1
            first = jnp.where(upper, partner, panel)
            second = jnp.where(upper, panel, partner)
            panel = jnp.concatenate([first, second], axis=0)
        return panel

    def apply_inverse(inverse, words, depth_bits):
        panel = collect(words, depth_bits)
        return jnp.dot(inverse, panel, preferred_element_type=jnp.float32)

    def halve_whole(current, depth_bits):
        for bit_index in reversed(range(depth_bits)):
            half = current.shape[0] // 2
            upper = leaf_index >> bit_index & 1 == 1
            keep = jnp.where(upper, current[half:], current[:half])
            give = jnp.where(upper, current[:half], current[half:])
            current = keep + from_partner(give, "leaf", bit_index)
        return current

    def reduce_slots(partial_value, depth_bits):
        current = halve_whole(partial_value, depth_bits)
        return lax.psum_scatter(current, "sep", scatter_dimension=0, tiled=True)

    def selector(targets, blocks):
        return (jnp.arange(blocks, dtype=jnp.int32)[:, None] == targets[0][None, :]).astype(
            jnp.float32
        )

    def place_slots(summed, targets, blocks):
        onehot = selector(targets, blocks)
        flat = summed.reshape(targets.shape[1], BLOCK * width)
        placed = jnp.dot(onehot, flat, precision=lax.Precision.HIGHEST)
        return placed.reshape(blocks * BLOCK, width)

    def pick_slots(table, targets, blocks):
        onehot = selector(targets, blocks)
        flat = table.astype(jnp.float32).reshape(blocks, BLOCK * width)
        picked = jnp.dot(onehot.T, flat, precision=lax.Precision.HIGHEST)
        return picked.reshape(targets.shape[1] * BLOCK, width).astype(jnp.bfloat16)

    contract_rows = (((0,), (0,)), ((), ()))
    lower_blocks = 2 * dev_rows // BLOCK
    middle_blocks = dev_rows // BLOCK
    lower_words = lower_side.astype(jnp.bfloat16)
    lower_values = apply_inverse(inverse_lower, lower_words, leaf_bits - 2)
    lower_partial = lax.dot_general(
        update_lower, lower_words, contract_rows, preferred_element_type=jnp.float32
    )
    lower_accum = place_slots(
        reduce_slots(lower_partial, leaf_bits - 2), target_lower, lower_blocks
    )
    middle_words = (middle_side - lower_accum[dev_rows:]).astype(jnp.bfloat16)
    middle_values = apply_inverse(inverse_middle, middle_words, leaf_bits - 1)
    middle_partial = lax.dot_general(
        update_middle, middle_words, contract_rows, preferred_element_type=jnp.float32
    )
    middle_accum = place_slots(
        reduce_slots(middle_partial, leaf_bits - 1), target_middle, middle_blocks
    )
    root_words = (root_side - (lower_accum[:dev_rows] + middle_accum)).astype(jnp.bfloat16)
    root_solution = apply_inverse(inverse_root, root_words, leaf_bits)
    root_rounded = root_solution.astype(jnp.bfloat16)
    middle_slots = collect(pick_slots(root_rounded, target_middle, middle_blocks), leaf_bits - 1)
    middle_solution = middle_values - jnp.dot(
        update_middle, middle_slots, preferred_element_type=jnp.float32
    )
    middle_rounded = middle_solution.astype(jnp.bfloat16)
    table = jnp.concatenate([root_rounded, middle_rounded], axis=0)
    lower_slots = collect(pick_slots(table, target_lower, lower_blocks), leaf_bits - 2)
    lower_solution = lower_values - jnp.dot(
        update_lower, lower_slots, preferred_element_type=jnp.float32
    )
    return jnp.concatenate([root_solution, middle_solution, lower_solution], axis=0)


def solution(mesh):
    in_specs = (
        P(("leaf", "sep"), None),
        P(("leaf", "sep"), None),
        P(("leaf", "sep"), None),
        P(("leaf", "sep"), None),
        P(("leaf", "sep"), None),
        P(("leaf", "sep"), None),
        P(("leaf", "sep"), None),
        P(("leaf", "sep"), None),
    )
    out_specs = P(("leaf", "sep"), None)
    return jax.shard_map(
        on_device, mesh=mesh, in_specs=in_specs, out_specs=out_specs, check_vma=False
    )
```

profile of v0, /device:TPU:0, one launch (start us, length us, event | category | flops | bytes accessed | tf_op | source)
XLA Modules:
  0.0 152.9 jit_solution(7578756123601498769)
XLA Ops:
  0.0 1.3 fusion.44
  1.3 3.0 %collective-permute-start = (f32[32,128]{1,0:T(8,128)S(1)}, f32[32,128]{1,0:T(8,128)S(1)}, u32[]{:S(2)}, u32[]{:S(2)}) collective-permute-start(f32[32,128]{1,0:T(8,128)S(1)} %slice_select_fusion.2), channel_id=1, source_target_pairs={{0,4},{4,0},{8,12},{12,8},{16,20},{20,16},{24,28},{28,24},{1,5},{5... | collective-permute-start | bytes 49160 | tf_op jit(solution)/shard_map/ppermute | solution.py:16
  5.0 1.2 dynamic-slice
  6.9 10.7 %all-reduce = f32[32,128]{1,0:T(8,128)S(1)} all-reduce(f32[32,128]{1,0:T(8,128)S(1)} %select_add_fusion.2), channel_id=2, replica_groups=mesh['leaf'=8,'sep'=4] {'sep'}, use_global_device_ids=true, to_apply=%region_0.1.clone | all-reduce | flops 4096 | bytes 32768
  18.6 1.1 convolution_bitcast_fusion
  19.7 1.6 %collective-permute-start.1 = (f32[64,128]{1,0:T(8,128)S(1)}, f32[64,128]{1,0:T(8,128)S(1)}, u32[]{:S(2)}, u32[]{:S(2)}) collective-permute-start(f32[64,128]{1,0:T(8,128)S(1)} %slice_select_fusion), channel_id=1, source_target_pairs={{0,8},{8,0},{4,12},{12,4},{16,24},{24,16},{20,28},{28,20},{1,9},{9... | collective-permute-start | bytes 98312 | tf_op jit(solution)/shard_map/ppermute | solution.py:16
  22.0 1.7 %collective-permute-done.1 = f32[64,128]{1,0:T(8,128)S(1)} collective-permute-done((f32[64,128]{1,0:T(8,128)S(1)}, f32[64,128]{1,0:T(8,128)S(1)}, u32[]{:S(2)}, u32[]{:S(2)}) %collective-permute-start.1) | collective-permute-done | bytes 32800 | tf_op jit(solution)/shard_map/ppermute | solution.py:16
  24.4 3.1 %collective-permute-done.2 = f32[32,128]{1,0:T(8,128)S(1)} collective-permute-done((f32[32,128]{1,0:T(8,128)S(1)}, f32[32,128]{1,0:T(8,128)S(1)}, u32[]{:S(2)}, u32[]{:S(2)}) %collective-permute-start.2) | collective-permute-done | bytes 16416 | tf_op jit(solution)/shard_map/ppermute | solution.py:16
  27.5 10.1 %all-reduce.1 = f32[32,128]{1,0:T(8,128)S(1)} all-reduce(f32[32,128]{1,0:T(8,128)S(1)} %select_add_fusion.1), channel_id=3, replica_groups=mesh['leaf'=8,'sep'=4] {'sep'}, use_global_device_ids=true, to_apply=%region_1.2.clone | all-reduce | flops 4096 | bytes 32768
  38.7 5.8 %all_gather.15 = bf16[1024,128]{1,0:T(8,128)(2,1)S(1)} all-gather(bf16[256,128]{1,0:T(8,128)(2,1)S(1)} %subtract_convert_fusion), channel_id=1, replica_groups=mesh['leaf'=8,'sep'=4] {'sep'}, dimensions={0}, use_global_device_ids=true | all-gather | bytes 327680 | tf_op jit(solution)/shard_map/all_gather | solution.py:39
  45.1 7.9 %collective-permute-done.3 = bf16[1024,128]{1,0:T(8,128)(2,1)S(1)} collective-permute-done((bf16[1024,128]{1,0:T(8,128)(2,1)S(1)}, bf16[1024,128]{1,0:T(8,128)(2,1)S(1)}, u32[]{:S(2)}, u32[]{:S(2)}) %collective-permute-start.3) | collective-permute-done | bytes 262176 | tf_op jit(solution)/shard_map/ppermute | solution.py:16
  53.1 1.6 %collective-permute-start.4 = (bf16[2048,128]{1,0:T(8,128)(2,1)S(1)}, bf16[2048,128]{1,0:T(8,128)(2,1)S(1)}, u32[]{:S(2)}, u32[]{:S(2)}) collective-permute-start(bf16[2048,128]{1,0:T(8,128)(2,1)S(1)} %pad_maximum_fusion.1), channel_id=1, source_target_pairs={{0,8},{8,0},{4,12},{12,4},{16,24},{24,16},{20,28},{28,20},{1,9},{9... | collective-permute-start | bytes 1572872 | tf_op jit(solution)/shard_map/ppermute | solution.py:16
  54.8 11.8 %collective-permute-done.4 = bf16[2048,128]{1,0:T(8,128)(2,1)S(1)} collective-permute-done((bf16[2048,128]{1,0:T(8,128)(2,1)S(1)}, bf16[2048,128]{1,0:T(8,128)(2,1)S(1)}, u32[]{:S(2)}, u32[]{:S(2)}) %collective-permute-start.4) | collective-permute-done | bytes 524320 | tf_op jit(solution)/shard_map/ppermute | solution.py:16
  66.8 1.1 pad_maximum_fusion
  67.8 2.6 %collective-permute-start.5 = (bf16[4096,128]{1,0:T(8,128)(2,1)}, bf16[4096,128]{1,0:T(8,128)(2,1)}, u32[]{:S(2)}, u32[]{:S(2)}) collective-permute-start(bf16[4096,128]{1,0:T(8,128)(2,1)} %pad_maximum_fusion), channel_id=1, source_target_pairs={{0,16},{16,0},{4,20},{20,4},{8,24},{24,8},{12,28},{28,12},{1,17},{... | collective-permute-start | bytes 3145736 | tf_op jit(solution)/shard_map/ppermute | solution.py:16
  70.4 5.8 %all_gather.16 = bf16[1024,128]{1,0:T(8,128)(2,1)S(1)} all-gather(bf16[256,128]{1,0:T(8,128)(2,1)S(1)} %subtract_convert_fusion.1), channel_id=1, replica_groups=mesh['leaf'=8,'sep'=4] {'sep'}, dimensions={0}, use_global_device_ids=true | all-gather | bytes 327680 | tf_op jit(solution)/shard_map/all_gather | solution.py:39
  77.9 7.0 %collective-permute-done.6 = bf16[1024,128]{1,0:T(8,128)(2,1)} collective-permute-done((bf16[1024,128]{1,0:T(8,128)(2,1)S(1)}, bf16[1024,128]{1,0:T(8,128)(2,1)}, u32[]{:S(2)}, u32[]{:S(2)}) %collective-permute-start.6) | collective-permute-done | bytes 262176 | tf_op jit(solution)/shard_map/ppermute | solution.py:16
  84.9 1.1 broadcast_select_fusion.9
  87.5 1.6 %collective-permute-start.7 = (bf16[2048,128]{1,0:T(8,128)(2,1)}, bf16[2048,128]{1,0:T(8,128)(2,1)}, u32[]{:S(2)}, u32[]{:S(2)}) collective-permute-start(bf16[2048,128]{1,0:T(8,128)(2,1)} %pad_maximum_fusion.2), channel_id=1, source_target_pairs={{0,8},{8,0},{4,12},{12,4},{16,24},{24,16},{20,28},{28,20},{1,9},{9... | collective-permute-start | bytes 1572872 | tf_op jit(solution)/shard_map/ppermute | solution.py:16
  89.1 26.3 %collective-permute-done.5 = bf16[4096,128]{1,0:T(8,128)(2,1)} collective-permute-done((bf16[4096,128]{1,0:T(8,128)(2,1)}, bf16[4096,128]{1,0:T(8,128)(2,1)}, u32[]{:S(2)}, u32[]{:S(2)}) %collective-permute-start.5) | collective-permute-done | bytes 1048608 | tf_op jit(solution)/shard_map/ppermute | solution.py:16
  115.3 1.6 %broadcast_select_fusion.1 = (bf16[4096,128]{1,0:T(8,128)(2,1)S(1)}, bf16[4096,128]{1,0:T(8,128)(2,1)S(1)}) fusion(bf16[4096,128]{1,0:T(8,128)(2,1)} %collective-permute-done.5, pred[]{:T(512)S(6)} %eq.94, bf16[2048,128]{1,0:T(8,128)(2,1)S(1)} %get-tuple-element.12, bf16[2048,128]{1,0:T(8,128)(2,1)S(1)} %get-tuple-element.11), kind=kLoop, calls=%fused_computation.18 | loop fusion | flops 3145728 | bytes 4194305 | tf_op jit(solution)/shard_map/jit(_where)/select_n | solution.py:43
  117.0 2.2 %fusion.42 = (bf16[256,128]{0,1:T(8,128)(2,1)S(1)}, f32[256,128]{0,1:T(8,128)}) fusion(bf16[256,8192]{1,0:T(8,128)(2,1)S(1)} %copy-done.7, bf16[4096,128]{1,0:T(8,128)(2,1)S(1)} %get-tuple-element.6, bf16[4096,128]{1,0:T(8,128)(2,1)S(1)} %get-tuple-element.5), kind=kOutput, calls=%fused_computation.82 | convolution fusion | flops 541097984 | bytes 6488064 | tf_op jit(solution)/shard_map/dot_general | solution.py:50
  119.5 5.2 %all_gather.17 = bf16[32,128]{1,0:T(8,128)(2,1)S(1)} all-gather(bf16[8,128]{1,0:T(8,128)(2,1)S(1)} %convert_element_type.28), channel_id=1, replica_groups=mesh['leaf'=8,'sep'=4] {'sep'}, dimensions={0}, use_global_device_ids=true | all-gather | bytes 10240 | tf_op jit(solution)/shard_map/all_gather | solution.py:39
  125.3 7.2 %all_gather.18 = bf16[2048,128]{1,0:T(8,128)(2,1)S(1)} all-gather(bf16[512,128]{1,0:T(8,128)(2,1)S(1)} %slice.81), channel_id=1, replica_groups=mesh['leaf'=8,'sep'=4] {'sep'}, dimensions={0}, use_global_device_ids=true | all-gather | bytes 655360 | tf_op jit(solution)/shard_map/all_gather | solution.py:39
  132.5 1.1 collective-permute-start.10
  134.3 1.2 broadcast_select_fusion.5
  135.5 1.9 %collective-permute-done.9 = bf16[64,128]{1,0:T(8,128)(2,1)S(1)} collective-permute-done((bf16[64,128]{1,0:T(8,128)(2,1)S(1)}, bf16[64,128]{1,0:T(8,128)(2,1)S(1)}, u32[]{:S(2)}, u32[]{:S(2)}) %collective-permute-start.9) | collective-permute-done | bytes 16416 | tf_op jit(solution)/shard_map/ppermute | solution.py:16
  138.9 5.2 %all_gather.19 = bf16[32,128]{1,0:T(8,128)(2,1)S(1)} all-gather(bf16[8,128]{1,0:T(8,128)(2,1)S(1)} %convert_element_type.30), channel_id=1, replica_groups=mesh['leaf'=8,'sep'=4] {'sep'}, dimensions={0}, use_global_device_ids=true | all-gather | bytes 10240 | tf_op jit(solution)/shard_map/all_gather | solution.py:39
  144.9 1.8 %collective-permute-done.10 = bf16[2048,128]{1,0:T(8,128)(2,1)} collective-permute-done((bf16[2048,128]{1,0:T(8,128)(2,1)S(1)}, bf16[2048,128]{1,0:T(8,128)(2,1)}, u32[]{:S(2)}, u32[]{:S(2)}) %collective-permute-start.10) | collective-permute-done | bytes 524320 | tf_op jit(solution)/shard_map/ppermute | solution.py:16
  146.8 1.1 broadcast_select_fusion.3
  148.1 3.8 %fusion.4 = f32[512,128]{0,1:T(8,128)S(1)} fusion(f32[128,512]{1,0:T(8,128)S(1)} %fusion.25, bf16[512,4096]{1,0:T(8,128)(2,1)} %param.11, bf16[2048,128]{1,0:T(8,128)(2,1)S(1)} %get-tuple-element.8, bf16[2048,128]{1,0:T(8,128)(2,1)S(1)} %get-tuple-element.7), kind=kOutput, calls=%fused_computation.5 | convolution fusion | flops 539033600 | bytes 5767168 | tf_op jit(solution)/shard_map/dot_general | solution.py:50
  152.0 1.0 copy.15
  (65 shorter events, 11.2 us)
Async XLA Ops:
  0.0 137.6 %copy-start = (bf16[256,4096]{1,0:T(8,128)(2,1)S(1)}, bf16[256,4096]{1,0:T(8,128)(2,1)}, u32[]{:S(2)}) copy-start(bf16[256,4096]{1,0:T(8,128)(2,1)} %param.10) | copy-start | bytes 6291460
  1.3 5.6 %collective-permute-start = (f32[32,128]{1,0:T(8,128)S(1)}, f32[32,128]{1,0:T(8,128)S(1)}, u32[]{:S(2)}, u32[]{:S(2)}) collective-permute-start(f32[32,128]{1,0:T(8,128)S(1)} %slice_select_fusion.2), channel_id=1, source_target_pairs={{0,4},{4,0},{8,12},{12,8},{16,20},{20,16},{24,28},{28,24},{1,5},{5... | collective-permute-start | bytes 49160 | tf_op jit(solution)/shard_map/ppermute | solution.py:16
  19.7 4.0 %collective-permute-start.1 = (f32[64,128]{1,0:T(8,128)S(1)}, f32[64,128]{1,0:T(8,128)S(1)}, u32[]{:S(2)}, u32[]{:S(2)}) collective-permute-start(f32[64,128]{1,0:T(8,128)S(1)} %slice_select_fusion), channel_id=1, source_target_pairs={{0,8},{8,0},{4,12},{12,4},{16,24},{24,16},{20,28},{28,20},{1,9},{9... | collective-permute-start | bytes 98312 | tf_op jit(solution)/shard_map/ppermute | solution.py:16
  23.7 3.8 %collective-permute-start.2 = (f32[32,128]{1,0:T(8,128)S(1)}, f32[32,128]{1,0:T(8,128)S(1)}, u32[]{:S(2)}, u32[]{:S(2)}) collective-permute-start(f32[32,128]{1,0:T(8,128)S(1)} %slice_select_fusion.1), channel_id=1, source_target_pairs={{0,4},{4,0},{8,12},{12,8},{16,20},{20,16},{24,28},{28,24},{1,5},{5... | collective-permute-start | bytes 49160 | tf_op jit(solution)/shard_map/ppermute | solution.py:16
  44.5 8.6 %collective-permute-start.3 = (bf16[1024,128]{1,0:T(8,128)(2,1)S(1)}, bf16[1024,128]{1,0:T(8,128)(2,1)S(1)}, u32[]{:S(2)}, u32[]{:S(2)}) collective-permute-start(bf16[1024,128]{1,0:T(8,128)(2,1)S(1)} %all_gather.15), channel_id=1, source_target_pairs={{0,4},{4,0},{8,12},{12,8},{16,20},{20,16},{24,28},{28,24},{1,5},{5... | collective-permute-start | bytes 786440 | tf_op jit(solution)/shard_map/ppermute | solution.py:16
  53.1 13.4 %collective-permute-start.4 = (bf16[2048,128]{1,0:T(8,128)(2,1)S(1)}, bf16[2048,128]{1,0:T(8,128)(2,1)S(1)}, u32[]{:S(2)}, u32[]{:S(2)}) collective-permute-start(bf16[2048,128]{1,0:T(8,128)(2,1)S(1)} %pad_maximum_fusion.1), channel_id=1, source_target_pairs={{0,8},{8,0},{4,12},{12,4},{16,24},{24,16},{20,28},{28,20},{1,9},{9... | collective-permute-start | bytes 1572872 | tf_op jit(solution)/shard_map/ppermute | solution.py:16
  67.8 47.5 %collective-permute-start.5 = (bf16[4096,128]{1,0:T(8,128)(2,1)}, bf16[4096,128]{1,0:T(8,128)(2,1)}, u32[]{:S(2)}, u32[]{:S(2)}) collective-permute-start(bf16[4096,128]{1,0:T(8,128)(2,1)} %pad_maximum_fusion), channel_id=1, source_target_pairs={{0,16},{16,0},{4,20},{20,4},{8,24},{24,8},{12,28},{28,12},{1,17},{... | collective-permute-start | bytes 3145736 | tf_op jit(solution)/shard_map/ppermute | solution.py:16
  76.2 1.6 %copy-start.3 = (bf16[1024,128]{1,0:T(8,128)(2,1)}, bf16[1024,128]{1,0:T(8,128)(2,1)S(1)}, u32[]{:S(2)}) copy-start(bf16[1024,128]{1,0:T(8,128)(2,1)S(1)} %all_gather.16) | copy-start | bytes 786436
  76.2 8.7 %collective-permute-start.6 = (bf16[1024,128]{1,0:T(8,128)(2,1)S(1)}, bf16[1024,128]{1,0:T(8,128)(2,1)}, u32[]{:S(2)}, u32[]{:S(2)}) collective-permute-start(bf16[1024,128]{1,0:T(8,128)(2,1)S(1)} %all_gather.16), channel_id=1, source_target_pairs={{0,4},{4,0},{8,12},{12,8},{16,20},{20,16},{24,28},{28,24},{1,5},{5... | collective-permute-start | bytes 786440 | tf_op jit(solution)/shard_map/ppermute | solution.py:16
  85.9 0.7 copy-start.1
  87.5 29.5 %copy-start.7 = (bf16[256,8192]{1,0:T(8,128)(2,1)S(1)}, bf16[256,8192]{1,0:T(8,128)(2,1)}, u32[]{:S(2)}) copy-start(bf16[256,8192]{1,0:T(8,128)(2,1)} %param.9) | copy-start | bytes 12582916
  87.5 46.8 %collective-permute-start.7 = (bf16[2048,128]{1,0:T(8,128)(2,1)}, bf16[2048,128]{1,0:T(8,128)(2,1)}, u32[]{:S(2)}, u32[]{:S(2)}) collective-permute-start(bf16[2048,128]{1,0:T(8,128)(2,1)} %pad_maximum_fusion.2), channel_id=1, source_target_pairs={{0,8},{8,0},{4,12},{12,4},{16,24},{24,16},{20,28},{28,20},{1,9},{9... | collective-permute-start | bytes 1572872 | tf_op jit(solution)/shard_map/ppermute | solution.py:16
  117.0 17.3 %copy-start.2 = (bf16[1024,128]{1,0:T(8,128)(2,1)S(1)}, bf16[1024,128]{1,0:T(8,128)(2,1)}, u32[]{:S(2)}) copy-start(bf16[1024,128]{1,0:T(8,128)(2,1)} %copy-done.1) | copy-start | bytes 786436
  119.2 18.3 %copy-start.4 = (bf16[256,128]{1,0:T(8,128)(2,1)S(1)}, bf16[256,128]{1,0:T(8,128)(2,1)}, u32[]{:S(2)}) copy-start(bf16[256,128]{1,0:T(8,128)(2,1)} %param.12) | copy-start | bytes 196612
  124.6 9.0 %collective-permute-start.8 = (bf16[32,128]{1,0:T(8,128)(2,1)S(1)}, bf16[32,128]{1,0:T(8,128)(2,1)S(1)}, u32[]{:S(2)}, u32[]{:S(2)}) collective-permute-start(bf16[32,128]{1,0:T(8,128)(2,1)S(1)} %all_gather.17), channel_id=1, source_target_pairs={{0,4},{4,0},{8,12},{12,8},{16,20},{20,16},{24,28},{28,24},{1,5},{5... | collective-permute-start | bytes 24584 | tf_op jit(solution)/shard_map/ppermute | solution.py:16
  132.5 14.3 %collective-permute-start.10 = (bf16[2048,128]{1,0:T(8,128)(2,1)S(1)}, bf16[2048,128]{1,0:T(8,128)(2,1)}, u32[]{:S(2)}, u32[]{:S(2)}) collective-permute-start(bf16[2048,128]{1,0:T(8,128)(2,1)S(1)} %all_gather.18), channel_id=1, source_target_pairs={{0,4},{4,0},{8,12},{12,8},{16,20},{20,16},{24,28},{28,24},{1,5},{5... | collective-permute-start | bytes 1572872 | tf_op jit(solution)/shard_map/ppermute | solution.py:16
  133.6 3.8 %collective-permute-start.9 = (bf16[64,128]{1,0:T(8,128)(2,1)S(1)}, bf16[64,128]{1,0:T(8,128)(2,1)S(1)}, u32[]{:S(2)}, u32[]{:S(2)}) collective-permute-start(bf16[64,128]{1,0:T(8,128)(2,1)S(1)} %pad_maximum_fusion.5), channel_id=1, source_target_pairs={{0,8},{8,0},{4,12},{12,4},{16,24},{24,16},{20,28},{28,20},{1,9},{9... | collective-permute-start | bytes 49160 | tf_op jit(solution)/shard_map/ppermute | solution.py:16
  138.5 9.4 %copy-start.5 = (bf16[512,64]{0,1:T(8,128)(2,1)S(1)}, bf16[512,64]{0,1:T(8,128)(2,1)}, u32[]{:S(2)}) copy-start(bf16[512,64]{0,1:T(8,128)(2,1)} %param.13) | copy-start | bytes 196612
  144.0 3.9 %collective-permute-start.11 = (bf16[32,128]{1,0:T(8,128)(2,1)S(1)}, bf16[32,128]{1,0:T(8,128)(2,1)S(1)}, u32[]{:S(2)}, u32[]{:S(2)}) collective-permute-start(bf16[32,128]{1,0:T(8,128)(2,1)S(1)} %all_gather.19), channel_id=1, source_target_pairs={{0,4},{4,0},{8,12},{12,8},{16,20},{20,16},{24,28},{28,24},{1,5},{5... | collective-permute-start | bytes 24584 | tf_op jit(solution)/shard_map/ppermute | solution.py:16
  148.1 3.8 %copy-start.6 = (f32[256,128]{0,1:T(8,128)S(1)}, f32[256,128]{0,1:T(8,128)}, u32[]{:S(2)}) copy-start(f32[256,128]{0,1:T(8,128)} %get-tuple-element.24) | copy-start | bytes 393220
where the time goes:
time: 154 us; the launch traced here: 153 us
  waiting for transfers between devices  61.5 us (40%)
  blocking collectives  49.8 us (32%)
  starting transfers between devices  15.8 us (10%)
  matrix products  9.76 us (6%)
  other arithmetic  9.43 us (6%)
  local copies, waits for them, and re-layouts  4.34 us (3%)
  between operations  2.28 us (1%)
    ppermute x12, waiting for transfers between devices, from_partner(): return lax.ppermute(block, axis, route)  61.5 us
    all_gather x5, blocking collectives, collect(): panel = lax.all_gather(piece, 'sep', axis=0, tiled=True)  29.1 us
    unnamed x2, blocking collectives  20.8 us
    ppermute x12, starting transfers between devices, from_partner(): return lax.ppermute(block, axis, route)  15.8 us
    dot_general x3, matrix products, apply_inverse(): return jnp.dot(inverse, panel, preferred_element_type=jnp.float32)  6.77 us
    select_n x9, other arithmetic, collect(): first = jnp.where(upper, partner, panel)  5.36 us
  transfers between devices with their start and end apart: 12, of which 8 were waited for; matrix products, arithmetic and copies ran while one was open for 8% of the time, Pallas kernels for 0%

commit v1 on v0

--- a/solution.py
+++ b/solution.py
@@ -1,6 +1,8 @@
 import jax
 import jax.numpy as jnp
 from jax import lax
+from jax.experimental import pallas as pl
+from jax.experimental.pallas import tpu as pltpu
 from jax.sharding import PartitionSpec as P
 
 BLOCK = 8
@@ -114,6 +116,341 @@
     return jnp.concatenate([root_solution, middle_solution, lower_solution], axis=0)
 
 
+PLANE = 8
+PAIR = 16
+PLANES = 4
+N_BULK = 8
+MESH = pl.DeviceIdType.MESH
+
+
+def fused_kernel(
+    side_hbm, root_hbm, middle_hbm, lower_hbm, up_mid_hbm, up_low_hbm, target_mid, target_low, out_hbm,
+    side, inv_root, inv_mid, inv_low, up_mid, up_low, low_panel, mid_panel, root_panel,
+    low_part, mid_part, low_in, mid_in, low_slots, mid_slots, xs,
+    load_sem, out_sem, small_send, small_recv, bulk_send, bulk_recv, z_send, z_recv,
+):
+    rows = root_hbm.shape[0]
+    plane_cols = PLANE * rows
+    leaf, sep = lax.axis_index("leaf"), lax.axis_index("sep")
+    z, x, y, c = leaf // 2, leaf % 2, sep // 2, sep % 2
+    z1, z2, z3 = z + 1 - 2 * (z % 2), (z + 2) % PLANES, PLANES - 1 - z
+    in_plane = x * 4 + sep
+    in_pair = (leaf % 4) * 4 + sep
+
+    def plane_peer(step):
+        peer = (in_plane + step) % PLANE
+        return peer, (z * 2 + peer // 4, peer % 4)
+
+    def pair_peer(step):
+        peer = (in_pair + step) % PAIR
+        return peer, (leaf // 4 * 4 + peer // 4, peer % 4)
+
+    x_peer = (z * 2 + 1 - x, sep)
+    y_peer = (leaf, (1 - y) * 2 + c)
+    sibling = (leaf, y * 2 + 1 - c)
+
+    barrier = pltpu.get_barrier_semaphore()
+    for step in range(1, PAIR):
+        pl.semaphore_signal(barrier, inc=1, device_id=pair_peer(step)[1], device_id_type=MESH)
+    for far in (z2, z3):
+        pl.semaphore_signal(barrier, inc=1, device_id=(far * 2 + x, sep), device_id_type=MESH)
+
+    loads = [
+        pltpu.make_async_copy(side_hbm.at[pl.ds(2 * rows, 2 * rows)], side.at[pl.ds(2 * rows, 2 * rows)], load_sem.at[0]),
+        pltpu.make_async_copy(up_low_hbm, up_low, load_sem.at[1]),
+        pltpu.make_async_copy(side_hbm.at[pl.ds(0, 2 * rows)], side.at[pl.ds(0, 2 * rows)], load_sem.at[2]),
+        pltpu.make_async_copy(up_mid_hbm, up_mid, load_sem.at[3]),
+        pltpu.make_async_copy(lower_hbm, inv_low, load_sem.at[4]),
+    ]
+    for half in range(2):
+        loads.append(
+            pltpu.make_async_copy(
+                middle_hbm.at[:, pl.ds(half * plane_cols, plane_cols)], inv_mid.at[half], load_sem.at[5 + half]
+            )
+        )
+    for plane in range(PLANES):
+        loads.append(
+            pltpu.make_async_copy(
+                root_hbm.at[:, pl.ds(plane * plane_cols, plane_cols)], inv_root.at[plane], load_sem.at[7 + plane]
+            )
+        )
+    for load in loads:
+        load.start()
+
+    started = []
+
+    def send(source, target, send_sem, recv_sem, device):
+        copy = pltpu.make_async_remote_copy(
+            src_ref=source, dst_ref=target, send_sem=send_sem, recv_sem=recv_sem,
+            device_id=device, device_id_type=MESH,
+        )
+        copy.start()
+        started.append(copy)
+
+    def arrived(ref, recv_sem):
+        pltpu.make_async_remote_copy(
+            src_ref=ref, dst_ref=ref, send_sem=small_send.at[0], recv_sem=recv_sem,
+            device_id=sibling, device_id_type=MESH,
+        ).wait_recv()
+
+    class Gather:
+        def __init__(self, panel, size, first, index):
+            self.panel, self.size, self.first, self.index = panel, size, first, index
+
+        def ref(self, px, py, pc, start=0, size=None):
+            where = (self.first + px * 4 + py * 2 + pc) * self.size + start
+            return self.panel.at[pl.ds(pl.multiple_of(where, 64), size or self.size)]
+
+        def sems(self, kind):
+            place = self.index * N_BULK + kind
+            return bulk_send.at[place], bulk_recv.at[place]
+
+        def copy(self, ref, kind, device):
+            send(ref, ref, *self.sems(kind), device)
+
+        def wait(self, ref, kind):
+            arrived(ref, self.sems(kind)[1])
+
+        def own(self):
+            ref = self.ref(x, y, c)
+            self.copy(ref, 0, x_peer)
+            self.copy(ref, 1, y_peer)
+            self.copy(ref, 2, sibling)
+
+        def pass_on(self):
+            half = self.size // 2
+            ref = self.ref(1 - x, y, c)
+            self.wait(ref, 0)
+            self.copy(self.ref(1 - x, y, c, 0, half), 3, y_peer)
+            self.copy(ref, 5, sibling)
+            ref = self.ref(x, 1 - y, c)
+            self.wait(ref, 1)
+            self.copy(self.ref(x, 1 - y, c, half, half), 4, x_peer)
+            self.copy(ref, 6, sibling)
+
+        def pass_far(self):
+            half = self.size // 2
+            self.wait(self.ref(1 - x, 1 - y, c, 0, half), 3)
+            self.wait(self.ref(1 - x, 1 - y, c, half, half), 4)
+            self.copy(self.ref(1 - x, 1 - y, c), 7, sibling)
+
+        def finish(self):
+            self.wait(self.ref(x, y, 1 - c), 2)
+            self.wait(self.ref(1 - x, y, 1 - c), 5)
+            self.wait(self.ref(x, 1 - y, 1 - c), 6)
+            self.wait(self.ref(1 - x, 1 - y, 1 - c), 7)
+
+    low = Gather(low_panel, 2 * rows, 0, 0)
+    mids = [Gather(mid_panel, rows, (zz % 2) * PLANE, 1 + i) for i, zz in enumerate((z, z1))]
+    roots = [Gather(root_panel, rows, zz * PLANE, 3 + i) for i, zz in enumerate((z, z1, z2, z3))]
+
+    contract = (((0,), (0,)), ((), ()))
+
+    def spread(block, position):
+        wide = jnp.broadcast_to(block[None], (rows // BLOCK,) + block.shape).reshape(rows, block.shape[1])
+        place = lax.broadcasted_iota(jnp.int32, wide.shape, 0) // BLOCK
+        return jnp.where(place == position, wide, 0.0)
+
+    loads[0].wait()
+    loads[1].wait()
+    low_words = side[2 * rows :, :].astype(jnp.bfloat16)
+    low.ref(x, y, c)[...] = low_words
+    low_part[...] = lax.dot_general(up_low[...], low_words, contract, preferred_element_type=jnp.float32)
+    pl.semaphore_wait(barrier, PAIR - 1 + 2)
+
+    def exchange(part, landing, count, peer_of, base):
+        for step in reversed(range(1, count)):
+            peer, device = peer_of(step)
+            source = part.at[pl.ds(pl.multiple_of(peer * BLOCK, BLOCK), BLOCK)]
+            send(source, landing.at[step], small_send.at[base + step], small_recv.at[base + step], device)
+
+    def collected(part, landing, count, mine, base):
+        total = part[pl.ds(pl.multiple_of(mine * BLOCK, BLOCK), BLOCK), :]
+        for step in range(1, count):
+            arrived(landing.at[step], small_recv.at[base + step])
+        for step in range(1, count):
+            total = total + landing[step]
+        return total
+
+    exchange(low_part, low_in, PLANE, plane_peer, 0)
+    low.own()
+    loads[2].wait()
+    loads[3].wait()
+    low_sum = collected(low_part, low_in, PLANE, in_plane, 0)
+
+    low_target = target_low[0, 0]
+    mid_target = target_mid[0, 0]
+    mid_words = (side[rows : 2 * rows, :] - spread(low_sum, low_target - rows // BLOCK)).astype(jnp.bfloat16)
+    mids[0].ref(x, y, c)[...] = mid_words
+    mid_part[...] = lax.dot_general(up_mid[...], mid_words, contract, preferred_element_type=jnp.float32)
+    exchange(mid_part, mid_in, PAIR, pair_peer, PLANE)
+    ref = mids[0].ref(x, y, c)
+    send(ref, ref, z_send.at[0], z_recv.at[0], (z1 * 2 + x, sep))
+    mids[0].own()
+    low.pass_on()
+    mid_sum = collected(mid_part, mid_in, PAIR, in_pair, PLANE)
+
+    root_words = (side[:rows, :] - (spread(low_sum, low_target) + spread(mid_sum, mid_target))).astype(jnp.bfloat16)
+    ref = roots[0].ref(x, y, c)
+    ref[...] = root_words
+    for i, zz in ((3, z3), (2, z2), (1, z1)):
+        send(ref, ref, z_send.at[i], z_recv.at[i], (zz * 2 + x, sep))
+    roots[0].own()
+
+    arrived(mids[1].ref(x, y, c), z_recv.at[0])
+    mids[1].own()
+    low.pass_far()
+    mids[0].pass_on()
+    arrived(roots[1].ref(x, y, c), z_recv.at[1])
+    roots[1].own()
+    low.finish()
+    loads[4].wait()
+
+    chunk = 1024
+    xs[2 * rows :, :] = jnp.zeros((2 * rows, xs.shape[1]), jnp.float32)
+
+    def low_step(first, last):
+        @pl.loop(first, last)
+        def _(i):
+            start = pl.multiple_of(i * chunk, chunk)
+            xs[2 * rows :, :] += jnp.dot(
+                inv_low[:, pl.ds(start, chunk)], low_panel[pl.ds(start, chunk), :],
+                preferred_element_type=jnp.float32,
+            )
+
+    chunks = low_panel.shape[0] // chunk
+    low_step(0, chunks // 2)
+    mids[1].pass_on()
+    mids[0].pass_far()
+    arrived(roots[2].ref(x, y, c), z_recv.at[2])
+    roots[2].own()
+    roots[0].pass_on()
+    arrived(roots[3].ref(x, y, c), z_recv.at[3])
+    roots[3].own()
+    low_step(chunks // 2, chunks)
+    mids[1].pass_far()
+    roots[1].pass_on()
+    roots[0].pass_far()
+    mids[0].finish()
+    mids[1].finish()
+    loads[5].wait()
+    loads[6].wait()
+    xs[rows : 2 * rows, :] = jnp.zeros((rows, xs.shape[1]), jnp.float32)
+    xs[:rows, :] = jnp.zeros((rows, xs.shape[1]), jnp.float32)
+
+    def mid_step(half):
+        start = half * plane_cols
+        xs[rows : 2 * rows, :] += jnp.dot(
+            inv_mid[half], mid_panel[start : start + plane_cols, :], preferred_element_type=jnp.float32
+        )
+
+    def root_step(gather, plane):
+        start = pl.multiple_of(plane * plane_cols, plane_cols)
+        xs[:rows, :] += jnp.dot(
+            inv_root[plane], root_panel[pl.ds(start, plane_cols), :], preferred_element_type=jnp.float32
+        )
+
+    mid_step(0)
+    roots[2].pass_on()
+    roots[1].pass_far()
+    mid_step(1)
+    roots[3].pass_on()
+    for plane in range(PLANES):
+        loads[7 + plane].wait()
+    roots[0].finish()
+    root_step(roots[0], z)
+    roots[2].pass_far()
+    roots[1].finish()
+    root_step(roots[1], z1)
+    roots[3].pass_far()
+    roots[2].finish()
+    root_step(roots[2], z2)
+    roots[3].finish()
+    root_step(roots[3], z3)
+
+    def share(slots, position, count, mine, peer_of, base):
+        rows_of = pl.ds(pl.multiple_of(mine * BLOCK, BLOCK), BLOCK)
+        table = xs[: 2 * rows, :].reshape(2 * rows // BLOCK, BLOCK, xs.shape[1])
+        place = lax.broadcasted_iota(jnp.int32, table.shape, 0)
+        slots[rows_of, :] = jnp.sum(jnp.where(place == position, table, 0.0), axis=0)
+        for step in reversed(range(1, count)):
+            send(slots.at[rows_of], slots.at[rows_of], small_send.at[base + step], small_recv.at[base + step], peer_of(step)[1])
+
+    def shared(slots, count, mine, base):
+        for step in range(1, count):
+            source = (mine + count - step) % count
+            arrived(slots.at[pl.ds(pl.multiple_of(source * BLOCK, BLOCK), BLOCK)], small_recv.at[base + step])
+        return slots[...].astype(jnp.bfloat16)
+
+    def store(piece, start, size):
+        copy = pltpu.make_async_copy(xs.at[pl.ds(start, size)], out_hbm.at[pl.ds(start, size)], out_sem.at[piece])
+        copy.start()
+        return copy
+
+    share(mid_slots, mid_target, PAIR, in_pair, pair_peer, PLANE + PAIR)
+    stores = [store(0, 0, rows)]
+    slots = shared(mid_slots, PAIR, in_pair, PLANE + PAIR)
+    xs[rows : 2 * rows, :] -= jnp.dot(up_mid[...], slots, preferred_element_type=jnp.float32)
+    share(low_slots, low_target, PLANE, in_plane, plane_peer, PLANE + 2 * PAIR)
+    stores.append(store(1, rows, rows))
+    slots = shared(low_slots, PLANE, in_plane, PLANE + 2 * PAIR)
+    xs[2 * rows :, :] -= jnp.dot(up_low[...], slots, preferred_element_type=jnp.float32)
+    stores.append(store(2, 2 * rows, 2 * rows))
+    for copy in started:
+        copy.wait_send()
+    for copy in stores:
+        copy.wait()
+
+
+def on_device_fused(
+    right_side, inverse_root, inverse_middle, inverse_lower, update_middle, update_lower, target_middle, target_lower
+):
+    rows = inverse_root.shape[0]
+    width = right_side.shape[1]
+    plane_cols = PLANE * rows
+    groups = 1 + 2 + PLANES
+    small = 2 * PLANE + 2 * PAIR
+    half, full = jnp.bfloat16, jnp.float32
+    dma = pltpu.SemaphoreType.DMA
+    hbm = pl.BlockSpec(memory_space=pl.ANY)
+    scalar = pl.BlockSpec(memory_space=pltpu.SMEM)
+    return pl.pallas_call(
+        fused_kernel,
+        out_shape=jax.ShapeDtypeStruct(right_side.shape, full),
+        in_specs=[hbm] * 6 + [scalar] * 2,
+        out_specs=hbm,
+        scratch_shapes=[
+            pltpu.VMEM(right_side.shape, full),
+            pltpu.VMEM((PLANES, rows, plane_cols), half),
+            pltpu.VMEM((2, rows, plane_cols), half),
+            pltpu.VMEM(inverse_lower.shape, half),
+            pltpu.VMEM(update_middle.shape, half),
+            pltpu.VMEM(update_lower.shape, half),
+            pltpu.VMEM((2 * rows * PLANE, width), half),
+            pltpu.VMEM((rows * PAIR, width), half),
+            pltpu.VMEM((rows * PLANE * PLANES, width), half),
+            pltpu.VMEM((PLANE * BLOCK, width), full),
+            pltpu.VMEM((PAIR * BLOCK, width), full),
+            pltpu.VMEM((PLANE, BLOCK, width), full),
+            pltpu.VMEM((PAIR, BLOCK, width), full),
+            pltpu.VMEM((PLANE * BLOCK, width), full),
+            pltpu.VMEM((PAIR * BLOCK, width), full),
+            pltpu.VMEM(right_side.shape, full),
+            dma((7 + PLANES,)),
+            dma((3,)),
+            dma((small,)),
+            dma((small,)),
+            dma((groups * N_BULK,)),
+            dma((groups * N_BULK,)),
+            dma((PLANES,)),
+            dma((PLANES,)),
+        ],
+        compiler_params=pltpu.CompilerParams(
+            collective_id=0, has_side_effects=True, vmem_limit_bytes=40 * 1024 * 1024
+        ),
+    )(right_side, inverse_root, inverse_middle, inverse_lower, update_middle, update_lower, target_middle, target_lower)
+
+
 def solution(mesh):
     in_specs = (
         P(("leaf", "sep"), None),
@@ -126,6 +463,7 @@
         P(("leaf", "sep"), None),
     )
     out_specs = P(("leaf", "sep"), None)
+    fits = dict(mesh.shape) == {"leaf": 8, "sep": 4}
     return jax.shard_map(
-        on_device, mesh=mesh, in_specs=in_specs, out_specs=out_specs, check_vma=False
-    )
+        on_device_fused if fits else on_device, mesh=mesh, in_specs=in_specs, out_specs=out_specs, check_vma=False
+    )

time: 154 us -> 51.9 us (0.34)
  waiting for transfers between devices: 61.5 us -> 0 us
  blocking collectives: 49.8 us -> 0 us
  Pallas kernels: 0 us -> 40.6 us
  starting transfers between devices: 15.8 us -> 0 us
  matrix products: 9.76 us -> 0 us
  other arithmetic: 9.43 us -> 0 us
  local copies, waits for them, and re-layouts: 4.34 us -> 9.6 us
    ppermute x12 -> x0, waiting for transfers between devices: 61.5 us -> none  [from_partner(): return lax.ppermute(block, axis, route)]
    pallas_call x0 -> x1, Pallas kernels: none -> 40.6 us  [on_device_fused(): pl.pallas_call(fused_kernel, out_shape=jax.ShapeDtypeStruct(right_side.sh...]
    all_gather x5 -> x0, blocking collectives: 29.1 us -> none  [collect(): panel = lax.all_gather(piece, 'sep', axis=0, tiled=True)]
    unnamed x2 -> x0, blocking collectives: 20.8 us -> none
    ppermute x12 -> x0, starting transfers between devices: 15.8 us -> none  [from_partner(): return lax.ppermute(block, axis, route)]
    dot_general x9 -> x0, matrix products: 9.76 us -> none  [the longest x3 6.77 us: apply_inverse(): return jnp.dot(inverse, panel, preferred_element_type=jnp.float32)]
    unnamed x17 -> x12, local copies, waits for them, and re-layouts: 1.98 us -> 9.6 us
    select_n x12 -> x0, other arithmetic: 5.38 us -> none  [the longest x9 5.36 us: collect(): first = jnp.where(upper, partner, panel)]
  transfers between devices with their start and end apart: 12 -> 0, of which waited for: 8 -> 0; matrix products, arithmetic and copies ran while one was open for 8% -> 0% of each run, Pallas kernels for 0% -> 0%
where the time goes in v1:
time: 51.9 us; the launch traced here: 51.5 us
  Pallas kernels  40.6 us (78%)
  local copies, waits for them, and re-layouts  9.6 us (18%)
  between operations  1.33 us (3%)
    pallas_call x1, Pallas kernels, on_device_fused(): pl.pallas_call(fused_kernel, out_shape=jax.ShapeDtypeStruct(right_side.sh...  40.6 us
    unnamed x12, local copies, waits for them, and re-layouts  9.6 us

profile of v1, /device:TPU:0, one launch (start us, length us, event | category | flops | bytes accessed | tf_op | source)
XLA Modules:
  0.0 51.5 jit_solution(1054083874494556682)
XLA Ops:
  1.3 1.0 %copy.9.up_low_hbm = bf16[512,64]{1,0:T(8,128)(2,1)S(1)} copy(bf16[512,64]{0,1:T(8,128)(2,1)} %param.13) | data formatting | bytes 131072 | tf_op args[5]
  2.3 0.0 copy-start
  2.3 2.2 %copy-done = bf16[256,8192]{1,0:T(8,128)(2,1)S(1)} copy-done((bf16[256,8192]{1,0:T(8,128)(2,1)S(1)}, bf16[256,8192]{1,0:T(8,128)(2,1)}, u32[]{:S(2)}) %copy-start) | copy-done | bytes 4194328
  4.5 0.0 copy-start.1
  4.5 2.2 %copy-done.1 = bf16[512,4096]{1,0:T(8,128)(2,1)S(1)} copy-done((bf16[512,4096]{1,0:T(8,128)(2,1)S(1)}, bf16[512,4096]{1,0:T(8,128)(2,1)}, u32[]{:S(2)}) %copy-start.1) | copy-done | bytes 4194328
  6.6 0.0 copy-start.2
  6.6 1.6 %copy-done.2 = bf16[256,4096]{1,0:T(8,128)(2,1)S(1)} copy-done((bf16[256,4096]{1,0:T(8,128)(2,1)S(1)}, bf16[256,4096]{1,0:T(8,128)(2,1)}, u32[]{:S(2)}) %copy-start.2) | copy-done | bytes 2097176
  8.2 0.0 copy-start.3
  8.2 1.0 %copy-done.3 = f32[1024,128]{1,0:T(8,128)S(1)} copy-done((f32[1024,128]{1,0:T(8,128)S(1)}, f32[1024,128]{1,0:T(8,128)}, u32[]{:S(2)}) %copy-start.3) | copy-done | bytes 524312
  9.3 0.0 copy-start.4
  9.3 0.8 %copy-done.4 = bf16[256,128]{1,0:T(8,128)(2,1)S(1)} copy-done((bf16[256,128]{1,0:T(8,128)(2,1)S(1)}, bf16[256,128]{1,0:T(8,128)(2,1)}, u32[]{:S(2)}) %copy-start.4) | copy-done | bytes 65560
  10.1 40.6 %shard_map.82 = f32[1024,128]{1,0:T(8,128)S(1)} custom-call(f32[1024,128]{1,0:T(8,128)S(1)} %copy-done.3, bf16[256,8192]{1,0:T(8,128)(2,1)S(1)} %copy-done, bf16[256,4096]{1,0:T(8,128)(2,1)S(1)} %copy-done.2, bf16[512,4096]{1,0:T(8,128)(2,1)S(1)} %copy-done.1, bf16[256,128]{1,0:T(8,128)(2,1)S(1)} %copy-done.4, bf16[512,64]{1,0:T(8,128)(2,1)S(1)} %copy.9.up_low_hbm, ...), custom_call_target="tpu_custom_call" | custom-call | tf_op jit(solution)/shard_map/pallas_call | solution.py:417
  50.7 0.8 %copy.13 = f32[1024,128]{1,0:T(8,128)} copy(f32[1024,128]{1,0:T(8,128)S(1)} %shard_map.82) | data formatting | bytes 1048576
Async XLA Ops:
  2.3 2.2 %copy-start = (bf16[256,8192]{1,0:T(8,128)(2,1)S(1)}, bf16[256,8192]{1,0:T(8,128)(2,1)}, u32[]{:S(2)}) copy-start(bf16[256,8192]{1,0:T(8,128)(2,1)} %root_hbm.1) | copy-start | bytes 12582916
  4.5 2.2 %copy-start.1 = (bf16[512,4096]{1,0:T(8,128)(2,1)S(1)}, bf16[512,4096]{1,0:T(8,128)(2,1)}, u32[]{:S(2)}) copy-start(bf16[512,4096]{1,0:T(8,128)(2,1)} %lower_hbm.1) | copy-start | bytes 12582916
  6.6 1.6 %copy-start.2 = (bf16[256,4096]{1,0:T(8,128)(2,1)S(1)}, bf16[256,4096]{1,0:T(8,128)(2,1)}, u32[]{:S(2)}) copy-start(bf16[256,4096]{1,0:T(8,128)(2,1)} %middle_hbm.1) | copy-start | bytes 6291460
  8.2 1.0 %copy-start.3 = (f32[1024,128]{1,0:T(8,128)S(1)}, f32[1024,128]{1,0:T(8,128)}, u32[]{:S(2)}) copy-start(f32[1024,128]{1,0:T(8,128)} %side_hbm.1) | copy-start | bytes 1572868
  9.3 0.8 %copy-start.4 = (bf16[256,128]{1,0:T(8,128)(2,1)S(1)}, bf16[256,128]{1,0:T(8,128)(2,1)}, u32[]{:S(2)}) copy-start(bf16[256,128]{1,0:T(8,128)(2,1)} %up_mid_hbm.1) | copy-start | bytes 196612

commit v2 on v1

--- a/solution.py
+++ b/solution.py
@@ -255,7 +255,7 @@
     loads[1].wait()
     low_words = side[2 * rows :, :].astype(jnp.bfloat16)
     low.ref(x, y, c)[...] = low_words
-    low_part[...] = lax.dot_general(up_low[...], low_words, contract, preferred_element_type=jnp.float32)
+    low_part[...] = jnp.dot(up_low[...], low_words, preferred_element_type=jnp.float32)
     pl.semaphore_wait(barrier, PAIR - 1 + 2)
 
     def exchange(part, landing, count, peer_of, base):
@@ -394,7 +394,7 @@
     share(low_slots, low_target, PLANE, in_plane, plane_peer, PLANE + 2 * PAIR)
     stores.append(store(1, rows, rows))
     slots = shared(low_slots, PLANE, in_plane, PLANE + 2 * PAIR)
-    xs[2 * rows :, :] -= jnp.dot(up_low[...], slots, preferred_element_type=jnp.float32)
+    xs[2 * rows :, :] -= lax.dot_general(up_low[...], slots, contract, preferred_element_type=jnp.float32)
     stores.append(store(2, 2 * rows, 2 * rows))
     for copy in started:
         copy.wait_send()
@@ -412,7 +412,7 @@
     small = 2 * PLANE + 2 * PAIR
     half, full = jnp.bfloat16, jnp.float32
     dma = pltpu.SemaphoreType.DMA
-    hbm = pl.BlockSpec(memory_space=pl.ANY)
+    hbm = pl.BlockSpec(memory_space=pltpu.HBM)
     scalar = pl.BlockSpec(memory_space=pltpu.SMEM)
     return pl.pallas_call(
         fused_kernel,
@@ -425,7 +425,7 @@
             pltpu.VMEM((2, rows, plane_cols), half),
             pltpu.VMEM(inverse_lower.shape, half),
             pltpu.VMEM(update_middle.shape, half),
-            pltpu.VMEM(update_lower.shape, half),
+            pltpu.VMEM(update_lower.shape[::-1], half),
             pltpu.VMEM((2 * rows * PLANE, width), half),
             pltpu.VMEM((rows * PAIR, width), half),
             pltpu.VMEM((rows * PLANE * PLANES, width), half),
@@ -446,9 +446,9 @@
             dma((PLANES,)),
         ],
         compiler_params=pltpu.CompilerParams(
-            collective_id=0, has_side_effects=True, vmem_limit_bytes=40 * 1024 * 1024
+            collective_id=0, has_side_effects=True, vmem_limit_bytes=60 * 1024 * 1024
         ),
-    )(right_side, inverse_root, inverse_middle, inverse_lower, update_middle, update_lower, target_middle, target_lower)
+    )(right_side, inverse_root, inverse_middle, inverse_lower, update_middle, update_lower.T, target_middle, target_lower)
 
 
 def solution(mesh):

time: 51.9 us -> 44.8 us (0.86)
  local copies, waits for them, and re-layouts: 9.6 us -> 1.87 us
  Pallas kernels: 40.6 us -> 41.5 us
    unnamed x12 -> x1, local copies, waits for them, and re-layouts: 9.6 us -> 1.87 us
    pallas_call x1, Pallas kernels: 40.6 us -> 41.5 us  [on_device_fused(): pl.pallas_call(fused_kernel, out_shape=jax.ShapeDtypeStruct(right_side.sh...]
where the time goes in v2:
time: 44.8 us; the launch traced here: 44.7 us
  Pallas kernels  41.5 us (93%)
  local copies, waits for them, and re-layouts  1.87 us (4%)
  between operations  1.3 us (3%)
    pallas_call x1, Pallas kernels, on_device_fused(): pl.pallas_call(fused_kernel, out_shape=jax.ShapeDtypeStruct(right_side.sh...  41.5 us
    unnamed x1, local copies, waits for them, and re-layouts  1.87 us

profile of v2, /device:TPU:0, one launch (start us, length us, event | category | flops | bytes accessed | tf_op | source)
XLA Modules:
  0.0 44.7 jit_solution(8437937907124085567)
XLA Ops:
  1.3 41.5 %shard_map.82 = f32[1024,128]{1,0:T(8,128)} custom-call(f32[1024,128]{1,0:T(8,128)} %side_hbm.1, bf16[256,8192]{1,0:T(8,128)(2,1)} %root_hbm.1, bf16[256,4096]{1,0:T(8,128)(2,1)} %middle_hbm.1, bf16[512,4096]{1,0:T(8,128)(2,1)} %lower_hbm.1, bf16[256,128]{1,0:T(8,128)(2,1)} %up_mid_hbm.1, bf16[64,512]{1,0:T(8,128)(2,1)} %bitcast.1, ...), custom_call_target="tpu_custom_call" | custom-call | tf_op jit(solution)/shard_map/pallas_call | solution.py:417
  42.8 1.9 %copy.12 = f32[1024,128]{1,0:T(8,128)} copy(f32[1024,128]{1,0:T(8,128)} %shard_map.82) | data formatting | bytes 1048576

commit v3 on v2

--- a/solution.py
+++ b/solution.py
@@ -126,7 +126,7 @@
 def fused_kernel(
     side_hbm, root_hbm, middle_hbm, lower_hbm, up_mid_hbm, up_low_hbm, target_mid, target_low, out_hbm,
     side, inv_root, inv_mid, inv_low, up_mid, up_low, low_panel, mid_panel, root_panel,
-    low_part, mid_part, low_in, mid_in, low_slots, mid_slots, xs,
+    low_part, mid_part, low_in, mid_in, hints, slots, xs,
     load_sem, out_sem, small_send, small_recv, bulk_send, bulk_recv, z_send, z_recv,
 ):
     rows = root_hbm.shape[0]
@@ -194,8 +194,9 @@
         ).wait_recv()
 
     class Gather:
-        def __init__(self, panel, size, first, index):
+        def __init__(self, panel, size, first, index, across=False):
             self.panel, self.size, self.first, self.index = panel, size, first, index
+            self.across = across
 
         def ref(self, px, py, pc, start=0, size=None):
             where = (self.first + px * 4 + py * 2 + pc) * self.size + start
@@ -211,8 +212,18 @@
         def wait(self, ref, kind):
             arrived(ref, self.sems(kind)[1])
 
+        def cross(self, ref, place):
+            if self.across:
+                send(ref, ref, z_send.at[PLANES + place], z_recv.at[PLANES + place], (z1 * 2 + x, sep))
+
+        def crossed(self, px, py, place, kind):
+            ref = self.ref(px, py, c)
+            arrived(ref, z_recv.at[PLANES + place])
+            self.copy(ref, kind, sibling)
+
         def own(self):
             ref = self.ref(x, y, c)
+            self.cross(ref, 0)
             self.copy(ref, 0, x_peer)
             self.copy(ref, 1, y_peer)
             self.copy(ref, 2, sibling)
@@ -222,17 +233,21 @@
             ref = self.ref(1 - x, y, c)
             self.wait(ref, 0)
             self.copy(self.ref(1 - x, y, c, 0, half), 3, y_peer)
+            self.cross(ref, 1)
             self.copy(ref, 5, sibling)
             ref = self.ref(x, 1 - y, c)
             self.wait(ref, 1)
             self.copy(self.ref(x, 1 - y, c, half, half), 4, x_peer)
+            self.cross(ref, 2)
             self.copy(ref, 6, sibling)
 
         def pass_far(self):
             half = self.size // 2
             self.wait(self.ref(1 - x, 1 - y, c, 0, half), 3)
             self.wait(self.ref(1 - x, 1 - y, c, half, half), 4)
-            self.copy(self.ref(1 - x, 1 - y, c), 7, sibling)
+            ref = self.ref(1 - x, 1 - y, c)
+            self.cross(ref, 3)
+            self.copy(ref, 7, sibling)
 
         def finish(self):
             self.wait(self.ref(x, y, 1 - c), 2)
@@ -241,7 +256,7 @@
             self.wait(self.ref(1 - x, 1 - y, 1 - c), 7)
 
     low = Gather(low_panel, 2 * rows, 0, 0)
-    mids = [Gather(mid_panel, rows, (zz % 2) * PLANE, 1 + i) for i, zz in enumerate((z, z1))]
+    mids = [Gather(mid_panel, rows, (zz % 2) * PLANE, 1 + i, i == 0) for i, zz in enumerate((z, z1))]
     roots = [Gather(root_panel, rows, zz * PLANE, 3 + i) for i, zz in enumerate((z, z1, z2, z3))]
 
     contract = (((0,), (0,)), ((), ()))
@@ -250,6 +265,11 @@
         wide = jnp.broadcast_to(block[None], (rows // BLOCK,) + block.shape).reshape(rows, block.shape[1])
         place = lax.broadcasted_iota(jnp.int32, wide.shape, 0) // BLOCK
         return jnp.where(place == position, wide, 0.0)
+
+    def pick(table, position):
+        blocks = table.reshape(rows // BLOCK, BLOCK, table.shape[1])
+        place = lax.broadcasted_iota(jnp.int32, blocks.shape, 0)
+        return jnp.sum(jnp.where(place == position, blocks, 0.0), axis=0)
 
     loads[0].wait()
     loads[1].wait()
@@ -284,8 +304,6 @@
     mids[0].ref(x, y, c)[...] = mid_words
     mid_part[...] = lax.dot_general(up_mid[...], mid_words, contract, preferred_element_type=jnp.float32)
     exchange(mid_part, mid_in, PAIR, pair_peer, PLANE)
-    ref = mids[0].ref(x, y, c)
-    send(ref, ref, z_send.at[0], z_recv.at[0], (z1 * 2 + x, sep))
     mids[0].own()
     low.pass_on()
     mid_sum = collected(mid_part, mid_in, PAIR, in_pair, PLANE)
@@ -297,8 +315,7 @@
         send(ref, ref, z_send.at[i], z_recv.at[i], (zz * 2 + x, sep))
     roots[0].own()
 
-    arrived(mids[1].ref(x, y, c), z_recv.at[0])
-    mids[1].own()
+    mids[1].crossed(x, y, 0, 2)
     low.pass_far()
     mids[0].pass_on()
     arrived(roots[1].ref(x, y, c), z_recv.at[1])
@@ -320,7 +337,6 @@
 
     chunks = low_panel.shape[0] // chunk
     low_step(0, chunks // 2)
-    mids[1].pass_on()
     mids[0].pass_far()
     arrived(roots[2].ref(x, y, c), z_recv.at[2])
     roots[2].own()
@@ -328,9 +344,11 @@
     arrived(roots[3].ref(x, y, c), z_recv.at[3])
     roots[3].own()
     low_step(chunks // 2, chunks)
-    mids[1].pass_far()
+    mids[1].crossed(1 - x, y, 1, 5)
+    mids[1].crossed(x, 1 - y, 2, 6)
     roots[1].pass_on()
     roots[0].pass_far()
+    mids[1].crossed(1 - x, 1 - y, 3, 7)
     mids[0].finish()
     mids[1].finish()
     loads[5].wait()
@@ -355,6 +373,13 @@
     roots[1].pass_far()
     mid_step(1)
     roots[3].pass_on()
+
+    own_hint = hints.at[in_plane]
+    own_hint[:BLOCK, :] = pick(xs[rows : 2 * rows, :], low_target - rows // BLOCK)
+    own_hint[BLOCK:, :] = pick(up_mid[...].astype(jnp.float32), low_target - rows // BLOCK)
+    for step in reversed(range(1, PLANE)):
+        at = PLANE + 2 * PAIR + step
+        send(own_hint, own_hint, small_send.at[at], small_recv.at[at], plane_peer(step)[1])
     for plane in range(PLANES):
         loads[7 + plane].wait()
     roots[0].finish()
@@ -368,34 +393,36 @@
     roots[3].finish()
     root_step(roots[3], z3)
 
-    def share(slots, position, count, mine, peer_of, base):
-        rows_of = pl.ds(pl.multiple_of(mine * BLOCK, BLOCK), BLOCK)
-        table = xs[: 2 * rows, :].reshape(2 * rows // BLOCK, BLOCK, xs.shape[1])
-        place = lax.broadcasted_iota(jnp.int32, table.shape, 0)
-        slots[rows_of, :] = jnp.sum(jnp.where(place == position, table, 0.0), axis=0)
-        for step in reversed(range(1, count)):
-            send(slots.at[rows_of], slots.at[rows_of], small_send.at[base + step], small_recv.at[base + step], peer_of(step)[1])
-
-    def shared(slots, count, mine, base):
-        for step in range(1, count):
-            source = (mine + count - step) % count
-            arrived(slots.at[pl.ds(pl.multiple_of(source * BLOCK, BLOCK), BLOCK)], small_recv.at[base + step])
-        return slots[...].astype(jnp.bfloat16)
-
     def store(piece, start, size):
         copy = pltpu.make_async_copy(xs.at[pl.ds(start, size)], out_hbm.at[pl.ds(start, size)], out_sem.at[piece])
         copy.start()
         return copy
 
-    share(mid_slots, mid_target, PAIR, in_pair, pair_peer, PLANE + PAIR)
+    own_slot = slots.at[in_pair]
+    own_slot[:BLOCK, :] = pick(xs[:rows, :], mid_target)
+    own_slot[BLOCK:, :] = pick(xs[:rows, :], low_target)
+    for step in reversed(range(1, PAIR)):
+        at = PLANE + PAIR + step
+        send(own_slot, own_slot, small_send.at[at], small_recv.at[at], pair_peer(step)[1])
     stores = [store(0, 0, rows)]
-    slots = shared(mid_slots, PAIR, in_pair, PLANE + PAIR)
-    xs[rows : 2 * rows, :] -= jnp.dot(up_mid[...], slots, preferred_element_type=jnp.float32)
-    share(low_slots, low_target, PLANE, in_plane, plane_peer, PLANE + 2 * PAIR)
+    for step in range(1, PLANE):
+        source = (in_plane + PLANE - step) % PLANE
+        arrived(hints.at[source], small_recv.at[PLANE + 2 * PAIR + step])
+    for step in range(1, PAIR):
+        source = (in_pair + PAIR - step) % PAIR
+        arrived(slots.at[source], small_recv.at[PLANE + PAIR + step])
+    width = xs.shape[1]
+    mid_slots = slots[:, :BLOCK, :].reshape(PAIR * BLOCK, width).astype(jnp.bfloat16)
+    low_base = slots[pl.ds(in_pair // PLANE * PLANE, PLANE), BLOCK:, :].reshape(PLANE * BLOCK, width)
+    hint_value = hints[:, :BLOCK, :].reshape(PLANE * BLOCK, width)
+    hint_update = hints[:, BLOCK:, :].reshape(PLANE * BLOCK, width).astype(jnp.bfloat16)
+    low_slots = low_base + (hint_value - jnp.dot(hint_update, mid_slots, preferred_element_type=jnp.float32))
+    xs[2 * rows :, :] -= lax.dot_general(
+        up_low[...], low_slots.astype(jnp.bfloat16), contract, preferred_element_type=jnp.float32
+    )
+    stores.append(store(2, 2 * rows, 2 * rows))
+    xs[rows : 2 * rows, :] -= jnp.dot(up_mid[...], mid_slots, preferred_element_type=jnp.float32)
     stores.append(store(1, rows, rows))
-    slots = shared(low_slots, PLANE, in_plane, PLANE + 2 * PAIR)
-    xs[2 * rows :, :] -= lax.dot_general(up_low[...], slots, contract, preferred_element_type=jnp.float32)
-    stores.append(store(2, 2 * rows, 2 * rows))
     for copy in started:
         copy.wait_send()
     for copy in stores:
@@ -433,8 +460,8 @@
             pltpu.VMEM((PAIR * BLOCK, width), full),
             pltpu.VMEM((PLANE, BLOCK, width), full),
             pltpu.VMEM((PAIR, BLOCK, width), full),
-            pltpu.VMEM((PLANE * BLOCK, width), full),
-            pltpu.VMEM((PAIR * BLOCK, width), full),
+            pltpu.VMEM((PLANE, 2 * BLOCK, width), full),
+            pltpu.VMEM((PAIR, 2 * BLOCK, width), full),
             pltpu.VMEM(right_side.shape, full),
             dma((7 + PLANES,)),
             dma((3,)),
@@ -442,8 +469,8 @@
             dma((small,)),
             dma((groups * N_BULK,)),
             dma((groups * N_BULK,)),
-            dma((PLANES,)),
-            dma((PLANES,)),
+            dma((2 * PLANES,)),
+            dma((2 * PLANES,)),
         ],
         compiler_params=pltpu.CompilerParams(
             collective_id=0, has_side_effects=True, vmem_limit_bytes=60 * 1024 * 1024

time: 44.8 us -> 42.8 us (0.955)
  Pallas kernels: 41.5 us -> 39.4 us
    pallas_call x1, Pallas kernels: 41.5 us -> 39.4 us  [on_device_fused(): pl.pallas_call(fused_kernel, out_shape=jax.ShapeDtypeStruct(right_side.sh...]
where the time goes in v3:
time: 42.8 us; the launch traced here: 42.6 us
  Pallas kernels  39.4 us (92%)
  local copies, waits for them, and re-layouts  1.87 us (4%)
  between operations  1.3 us (3%)
    pallas_call x1, Pallas kernels, on_device_fused(): pl.pallas_call(fused_kernel, out_shape=jax.ShapeDtypeStruct(right_side.sh...  39.4 us
    unnamed x1, local copies, waits for them, and re-layouts  1.87 us

profile of v3, /device:TPU:0, one launch (start us, length us, event | category | flops | bytes accessed | tf_op | source)
XLA Modules:
  0.0 42.6 jit_solution(11494077737070965514)
XLA Ops:
  1.3 39.4 %shard_map.82 = f32[1024,128]{1,0:T(8,128)} custom-call(f32[1024,128]{1,0:T(8,128)} %side_hbm.1, bf16[256,8192]{1,0:T(8,128)(2,1)} %root_hbm.1, bf16[256,4096]{1,0:T(8,128)(2,1)} %middle_hbm.1, bf16[512,4096]{1,0:T(8,128)(2,1)} %lower_hbm.1, bf16[256,128]{1,0:T(8,128)(2,1)} %up_mid_hbm.1, bf16[64,512]{1,0:T(8,128)(2,1)} %bitcast.1, ...), custom_call_target="tpu_custom_call" | custom-call | tf_op jit(solution)/shard_map/pallas_call | solution.py:444
  40.7 1.9 %copy.12 = f32[1024,128]{1,0:T(8,128)} copy(f32[1024,128]{1,0:T(8,128)} %shard_map.82) | data formatting | bytes 1048576

commit v4 on v3

--- a/solution.py
+++ b/solution.py
@@ -311,7 +311,7 @@
     root_words = (side[:rows, :] - (spread(low_sum, low_target) + spread(mid_sum, mid_target))).astype(jnp.bfloat16)
     ref = roots[0].ref(x, y, c)
     ref[...] = root_words
-    for i, zz in ((3, z3), (2, z2), (1, z1)):
+    for i, zz in ((1, z1), (2, z2), (3, z3)):
         send(ref, ref, z_send.at[i], z_recv.at[i], (zz * 2 + x, sep))
     roots[0].own()
 

time: 42.8 us -> 41.4 us (0.967)
  Pallas kernels: 39.4 us -> 38.1 us
    pallas_call x1, Pallas kernels: 39.4 us -> 38.1 us  [on_device_fused(): pl.pallas_call(fused_kernel, out_shape=jax.ShapeDtypeStruct(right_side.sh...]
where the time goes in v4:
time: 41.4 us; the launch traced here: 41.3 us
  Pallas kernels  38.1 us (92%)
  local copies, waits for them, and re-layouts  1.87 us (5%)
  between operations  1.3 us (3%)
    pallas_call x1, Pallas kernels, on_device_fused(): pl.pallas_call(fused_kernel, out_shape=jax.ShapeDtypeStruct(right_side.sh...  38.1 us
    unnamed x1, local copies, waits for them, and re-layouts  1.87 us

profile of v4, /device:TPU:0, one launch (start us, length us, event | category | flops | bytes accessed | tf_op | source)
XLA Modules:
  0.0 41.3 jit_solution(17082736241202272586)
XLA Ops:
  1.3 38.1 %shard_map.82 = f32[1024,128]{1,0:T(8,128)} custom-call(f32[1024,128]{1,0:T(8,128)} %side_hbm.1, bf16[256,8192]{1,0:T(8,128)(2,1)} %root_hbm.1, bf16[256,4096]{1,0:T(8,128)(2,1)} %middle_hbm.1, bf16[512,4096]{1,0:T(8,128)(2,1)} %lower_hbm.1, bf16[256,128]{1,0:T(8,128)(2,1)} %up_mid_hbm.1, bf16[64,512]{1,0:T(8,128)(2,1)} %bitcast.1, ...), custom_call_target="tpu_custom_call" | custom-call | tf_op jit(solution)/shard_map/pallas_call | solution.py:444
  39.4 1.9 %copy.12 = f32[1024,128]{1,0:T(8,128)} copy(f32[1024,128]{1,0:T(8,128)} %shard_map.82) | data formatting | bytes 1048576
